TPU v7x, 32 devices: a whole 2x2x4 slice. The times are simulated.
32 devices in a mesh: row: 4 (over x, core), sector: 4 (over z), band: 2 (over y).
Axes of the slice: x: 2, y: 2, z: 4, core: 2. Of those that a mesh axis runs over, the one named last changes fastest.
Arguments:
- residual: float32 [4, 4, 2, 320, 128], P('row', 'sector', 'band'), may hold values from -8 to 8
- block_inverse: float32 [4, 4, 2, 320, 320], P('row', 'sector', 'band'), may hold values from -0.3125 to 0.3125
- cycle_coupling: float32 [4, 4, 320, 320], P('row', 'sector'), as said below
- outlet_flux: float32 [4, 4, 2, 80, 320], P('row', 'sector', 'band'), may hold values from -0.3125 to 0.3125
- inlet_lift: float32 [4, 4, 2, 320, 80], P('row', 'sector', 'band'), may hold values from -0.5 to 0.5
- mortar_shift: int32 [3], replicated, may hold values from 0 to 3
Outputs:
- correction: float32 [4, 4, 2, 320, 128], P('row', 'sector', 'band')
- outlet_traces: float32 [4, 4, 2, 80, 128], P('row', 'sector', 'band')
Inputs may be any that keep to these rules, and one draw needn't show every extreme that they name: `mortar_shift`: one sector shift for each of the 3 interfaces between consecutive rows. `cycle_coupling`: each matrix is a positive diagonal plus full off-diagonal entries.
All inputs are finite; a program needn't handle non-finite values.
Results may differ from a plain program's by a relative error of at most 0.00017.
Values sent between devices are 32-bit elements; how exact they have to be, the bound alone decides.
A program may use at most 64 MiB of HBM per device.

v0:
```python
import functools

import jax
import jax.numpy as jnp
from jax import lax
from jax.experimental import pallas as pl
from jax.experimental.pallas import tpu as pltpu
from jax.sharding import PartitionSpec as P

HIGH = lax.Precision.HIGHEST
MESH = pl.DeviceIdType.MESH
F32 = jnp.float32
BF16 = jnp.bfloat16
RING_LIMIT = 8
QUARTERS = 4


def split(value):
    top = value.astype(BF16)
    return top, (value - top.astype(F32)).astype(BF16)


def dot(a, b):
    return jnp.dot(a, b, preferred_element_type=F32)


def times(a_top, a_rest, b):
    b_top, b_rest = split(b)
    width = b.shape[1]
    wide = dot(a_top, jnp.concatenate([b_top, b_rest], axis=1))
    return wide[:, :width] + (wide[:, width:] + dot(a_rest, b_top))


def keep(ref, matrix):
    depth = matrix.shape[1]
    top, rest = split(matrix)
    ref[:, :depth] = top
    ref[:, depth : 2 * depth] = top
    ref[:, 2 * depth :] = rest


def product(kept, b):
    top, rest = split(b)
    return dot(kept[...], jnp.concatenate([top, rest, top], axis=0))


def turn_lanes(value, by):
    by %= value.shape[1]
    return pltpu.roll(value, by, axis=1) if by else value


def pack(value, parts):
    high, width = value.shape[0] // parts, value.shape[1] // parts
    lane = lax.broadcasted_iota(jnp.int32, (high, value.shape[1]), 1)
    out = value[:high]
    for i in range(1, parts):
        block = turn_lanes(value[i * high : (i + 1) * high], i * width)
        out = jnp.where(lane < i * width, out, block)
    return out


def spread(value, parts, at=0):
    width = value.shape[1] // parts
    return jnp.concatenate(
        [turn_lanes(value, (at - i) * width) for i in range(parts)], axis=0
    )


def join(left, right, width):
    lane = lax.broadcasted_iota(jnp.int32, left.shape, 1)
    return jnp.where(lane < width, left, right)


def ring_kernel(
    sectors,
    shift_hbm, res_hbm, inv_hbm, coup_hbm, flux_hbm, lift_hbm,
    corr_ref, out_ref,
    shift_ref, res, inv, coup, flux, lift, coup3, flux3, flow3, lift3, cross3, other3_a, other3_b,
    source, seen, state, landed, solved, trace, face_trace, final, above_a, above_b, beside_a, beside_b, crosses, stage, given,
    load_sem, send_sem, recv_sem, above_recv, beside_recv, trace_send,
    cross_send, cross_recv, stage_send, given_recv,
):
    row = lax.axis_index("row")
    sector = lax.axis_index("sector")
    above, beside, other3 = (above_a, above_b), (beside_a, beside_b), (other3_a, other3_b)
    lines = res.shape[1]
    quarter, half = lines // QUARTERS, lines // 2

    def turn(k):
        return lax.rem(sector + k, sectors)

    def remote(src, dst, send, recv, down, k):
        return pltpu.make_async_remote_copy(
            src_ref=src, dst_ref=dst, send_sem=send, recv_sem=recv,
            device_id={"row": row + down, "sector": turn(k)}, device_id_type=MESH,
        )

    pairs = [
        (flux_hbm, flux), (lift_hbm, lift), (inv_hbm, inv), (res_hbm, res), (coup_hbm, coup),
        (shift_hbm, shift_ref),
    ]
    loads = [
        pltpu.make_async_copy(src, dst, load_sem.at[i]) for i, (src, dst) in enumerate(pairs)
    ]
    for load in loads:
        load.start()

    barrier = pltpu.get_barrier_semaphore()

    def greet(up, k):
        pl.semaphore_signal(
            barrier, inc=1, device_id={"row": row - up, "sector": turn(k)}, device_id_type=MESH
        )

    greet(0, sectors - 1)

    @pl.when(row == 1)
    def _():
        for k in range(1, sectors - 1):
            greet(0, k)

    @pl.when(row % 2 == 1)
    def _():
        for k in range(sectors):
            greet(1, k)

    @pl.when(row >= 2)
    def _():
        greet(row - 1, 0)

    loads[0].wait()
    loads[1].wait()
    crosses[sector] = times(*split(flux[...]), lift[...].T)

    @pl.when(row % 2 == 0)
    def _():
        pl.semaphore_wait(barrier, sectors + 1)

    @pl.when(row == 1)
    def _():
        pl.semaphore_wait(barrier, sectors + 1)

    @pl.when(row == 3)
    def _():
        pl.semaphore_wait(barrier, 1)

    def cross_copies():
        return (
            lambda: [
                remote(crosses.at[sector], crosses.at[sector], cross_send.at[k], cross_recv.at[sector], 0, k)
                for k in range(1, sectors)
            ],
            lambda: [
                remote(crosses.at[sector], above_cross(sector), cross_send.at[k], cross_recv.at[sector], 1, k)
                for k in range(sectors)
            ],
        )

    def above_cross(k):
        return crosses.at[sectors + k]

    @pl.when(row == 1)
    def _():
        for copy in cross_copies()[0]():
            copy.start()

    @pl.when(row == 2)
    def _():
        for copy in cross_copies()[1]():
            copy.start()

    steps = sectors - 1

    def ring_copy(k, q):
        return remote(
            state.at[k, q], landed.at[k, q], send_sem.at[k, q], recv_sem.at[k, q], 0, 1
        )

    loads[2].wait()
    loads[3].wait()
    source[...] = times(*split(inv[...]), res[...])
    for q in range(QUARTERS):
        state[0, q] = pack(turn_lanes(source[...], -q * quarter), QUARTERS)
        ring_copy(0, q).start()

    loads[4].wait()
    keep(coup3, coup[...])
    loads[5].wait()
    shift = [shift_ref[i] for i in range(3)]

    def back(by):
        return lax.rem(sector + 2 * sectors - by, sectors)

    def ready_flux():
        keep(flux3, flux[...])
        seen[...] = product(flux3, source[...])

    def ready_flow():
        keep(flow3, times(*split(flux[...]), coup[...]))

    def ready_lift():
        keep(lift3, lift[...].T)
        keep(cross3, crosses[sector])

    def ready_other():
        @pl.when(row == 1)
        def _():
            for i in range(1, sectors):
                remote(
                    crosses.at[turn(i)], crosses.at[turn(i)], cross_send.at[i],
                    cross_recv.at[turn(i)], 0, i,
                ).wait_recv()
            keep(other3[0], crosses[back(shift[1])])
            keep(other3[1], crosses[back(shift[1] + shift[2])])

        @pl.when(row == 3)
        def _():
            for i in range(sectors):
                remote(
                    crosses.at[0], above_cross(i), cross_send.at[i], cross_recv.at[i], -1, i
                ).wait_recv()
            keep(other3[0], crosses[sectors + back(shift[2])])

    aside = [ready_flux, ready_flow, ready_lift, ready_other]

    def trace_copies(h):
        return (
            lambda: [
                remote(trace.at[h], above[h].at[sector], trace_send.at[h, k], above_recv.at[h, sector], 1, k)
                for k in range(sectors)
            ],
            lambda: [
                remote(trace.at[h], beside[h].at[sector], trace_send.at[h, k], beside_recv.at[h, sector], 0, k)
                for k in range(1, sectors)
            ],
        )

    for k in range(steps - 1):
        for q in range(QUARTERS):
            ring_copy(k, q).wait_recv()
            came = product(coup3, spread(landed[k, q], QUARTERS))
            state[k + 1, q] = state[0, q] + pack(came, QUARTERS)
            ring_copy(k + 1, q).start()
            if aside:
                aside.pop(0)()
    while aside:
        aside.pop(0)()

    def here(value, h):
        return turn_lanes(value, h * half)

    for h in range(2):
        each = range(h * QUARTERS // 2, (h + 1) * QUARTERS // 2)
        came = None
        for at, q in enumerate(each):
            ring_copy(steps - 1, q).wait_recv()
            more = spread(landed[steps - 1, q], QUARTERS, at)
            came = more if came is None else join(came, more, at * quarter)
        face_trace[h] = here(seen[...], h) + product(flow3, came)
        trace[h] = pack(face_trace[h], 2)

        @pl.when(row % 2 == 0)
        def _():
            for copy in trace_copies(h)[0]():
                copy.start()

        @pl.when(row == 1)
        def _():
            for copy in trace_copies(h)[1]():
                copy.start()

        solved[h] = here(source[...], h) + product(coup3, came)

    def wait_above(h):
        for i in range(sectors):
            remote(
                trace.at[h], above[h].at[i], trace_send.at[h, 0], above_recv.at[h, i], -1, i
            ).wait_recv()

    def stage_copy(h, i):
        return remote(
            stage.at[h, i], given.at[h], stage_send.at[h, i], given_recv.at[h], i + 1, 0
        )

    def finish(h, moved):
        moved = spread(moved, 2)
        final[h] = face_trace[h] + product(cross3, moved)
        solved[h] += product(lift3, moved)

    @pl.when(row == 0)
    def _():
        final[...] = face_trace[...]

    @pl.when(row == 1)
    def _():
        for h in range(2):
            wait_above(h)
            for i in range(1, sectors):
                remote(
                    trace.at[h], beside[h].at[turn(i)], trace_send.at[h, i],
                    beside_recv.at[h, turn(i)], 0, i,
                ).wait_recv()
            beside[h][sector] = trace[h]
            for i, by in enumerate((shift[1], shift[1] + shift[2])):
                moved = above[h][lax.rem(back(by) + sectors - shift[0], sectors)]
                stage[h, i] = beside[h][back(by)] + pack(product(other3[i], spread(moved, 2)), 2)
                stage_copy(h, i).start()
        for h in range(2):
            finish(h, above[h][back(shift[0])])

    @pl.when(row == 2)
    def _():
        for h in range(2):
            stage_copy(h, 0).wait_recv()
            finish(h, given[h])

    @pl.when(row == 3)
    def _():
        for h in range(2):
            wait_above(h)
            stage_copy(h, 1).wait_recv()
            moved = above[h][back(shift[2])] + pack(product(other3[0], spread(given[h], 2)), 2)
            finish(h, moved)

    corr_ref[...] = join(solved[0], here(solved[1], 1), half)
    out_ref[...] = join(final[0], here(final[1], 1), half)

    for k in range(steps):
        for q in range(QUARTERS):
            ring_copy(k, q).wait_send()

    @pl.when(row % 2 == 0)
    def _():
        for h in range(2):
            for copy in trace_copies(h)[0]():
                copy.wait_send()

    @pl.when(row == 1)
    def _():
        for copy in cross_copies()[0]():
            copy.wait_send()
        for h in range(2):
            for copy in trace_copies(h)[1]():
                copy.wait_send()
            for i in range(2):
                stage_copy(h, i).wait_send()

    @pl.when(row == 2)
    def _():
        for copy in cross_copies()[1]():
            copy.wait_send()


def leave_kernel(corr_ref, out_ref, corr_hbm, out_hbm, sems):
    copies = [
        pltpu.make_async_copy(corr_ref, corr_hbm, sems.at[0]),
        pltpu.make_async_copy(out_ref, out_hbm, sems.at[1]),
    ]
    for copy in copies:
        copy.start()
    for copy in copies:
        copy.wait()


def ring_device(residual, block_inverse, cycle_coupling, outlet_flux, inlet_lift, mortar_shift):
    blk, lines = residual.shape[-2:]
    face = outlet_flux.shape[-2]
    sectors = lax.axis_size("sector")
    steps = sectors - 1
    vmem = pl.BlockSpec(memory_space=pltpu.VMEM)
    hbm = pl.BlockSpec(memory_space=pl.ANY)
    dma = pltpu.SemaphoreType.DMA
    corr, out = pl.pallas_call(
        functools.partial(ring_kernel, sectors),
        out_shape=(pltpu.VMEM((blk, lines), F32), pltpu.VMEM((face, lines), F32)),
        in_specs=[hbm] * 6,
        out_specs=(vmem, vmem),
        scratch_shapes=[
            pltpu.SMEM(mortar_shift.shape, jnp.int32),
            pltpu.VMEM((blk, lines), F32),
            pltpu.VMEM((blk, blk), F32),
            pltpu.VMEM((blk, blk), F32),
            pltpu.VMEM((face, blk), F32),
            pltpu.VMEM((face, blk), F32),
            pltpu.VMEM((blk, 3 * blk), BF16),
            pltpu.VMEM((face, 3 * blk), BF16),
            pltpu.VMEM((face, 3 * blk), BF16),
            pltpu.VMEM((blk, 3 * face), BF16),
            pltpu.VMEM((face, 3 * face), BF16),
            pltpu.VMEM((face, 3 * face), BF16),
            pltpu.VMEM((face, 3 * face), BF16),
            pltpu.VMEM((blk, lines), F32),
            pltpu.VMEM((face, lines), F32),
            pltpu.VMEM((steps, QUARTERS, blk // QUARTERS, lines), F32),
            pltpu.VMEM((steps, QUARTERS, blk // QUARTERS, lines), F32),
            pltpu.VMEM((2, blk, lines), F32),
            pltpu.VMEM((2, face // 2, lines), F32),
            pltpu.VMEM((2, face, lines), F32),
            pltpu.VMEM((2, face, lines), F32),
            pltpu.VMEM((sectors, face // 2, lines), F32),
            pltpu.VMEM((sectors, face // 2, lines), F32),
            pltpu.VMEM((sectors, face // 2, lines), F32),
            pltpu.VMEM((sectors, face // 2, lines), F32),
            pltpu.VMEM((2 * sectors, face, face), F32),
            pltpu.VMEM((2, 2, face // 2, lines), F32),
            pltpu.VMEM((2, face // 2, lines), F32),
            dma((6,)),
            dma((steps, QUARTERS)),
            dma((steps, QUARTERS)),
            dma((2, sectors)),
            dma((2, sectors)),
            dma((2, sectors)),
            dma((sectors,)),
            dma((sectors,)),
            dma((2, 2)),
            dma((2,)),
        ],
        compiler_params=pltpu.CompilerParams(
            collective_id=0, has_side_effects=True, vmem_limit_bytes=62 * 2**20
        ),
        name="ring",
    )(
        mortar_shift,
        residual.reshape(blk, lines),
        block_inverse.reshape(blk, blk),
        cycle_coupling.reshape(blk, blk),
        outlet_flux.reshape(face, blk),
        jnp.swapaxes(inlet_lift, -1, -2).reshape(face, blk),
    )
    corr, out = pl.pallas_call(
        leave_kernel,
        out_shape=(
            jax.ShapeDtypeStruct((blk, lines), F32),
            jax.ShapeDtypeStruct((face, lines), F32),
        ),
        in_specs=[hbm, hbm],
        out_specs=(hbm, hbm),
        scratch_shapes=[dma((2,))],
        compiler_params=pltpu.CompilerParams(vmem_limit_bytes=2**20),
        name="leave",
    )(corr, out)
    return corr.reshape(residual.shape), out.reshape(outlet_flux.shape[:-1] + (lines,))


def from_behind(block, axis, distance):
    devices = range(lax.axis_size(axis))
    route = [((i - distance) % len(devices), i) for i in devices]
    return lax.ppermute(block, axis, route)


def from_behind_2(value, axis, steps):
    count = lax.axis_size(axis)
    leading, last = (max(0, -steps), min(count, count - steps))
    return lax.ppermute(value, axis, [(source, source + steps) for source in range(leading, last)])


def apply_block(matrix, state):
    return jnp.einsum("ij,bjl->bil", matrix, state, precision=HIGH)


def turn_sectors(trace, offset, levels):
    for level in range(levels):
        moved = from_behind(trace, "sector", 2**level)
        trace = jnp.where(offset // 2**level % 2 == 1, moved, trace)
    return trace


def pass_down(trace):
    return from_behind_2(trace, "row", 1)


def doubling_device(residual, block_inverse, cycle_coupling, outlet_flux, inlet_lift, mortar_shift):
    res_local = residual[0, 0]
    inverse = block_inverse[0, 0]
    coupling = cycle_coupling[0, 0]
    flux = outlet_flux[0, 0]
    lift = inlet_lift[0, 0]
    source = jnp.einsum("bij,bjl->bil", inverse, res_local, precision=HIGH)
    levels = lax.axis_size("sector").bit_length() - 1
    matrix = coupling
    state = source
    for level in range(levels):
        if level + 1 < levels:
            prev_matrix, prev_state = from_behind((matrix, state), "sector", 2**level)
            state = state + apply_block(matrix, prev_state)
            matrix = jnp.dot(matrix, prev_matrix, precision=HIGH)
        else:
            prev_state = from_behind(state, "sector", 2**level)
            state = state + apply_block(matrix, prev_state)
    row_count = lax.axis_size("row")
    row_index = lax.axis_index("row")
    offset = jnp.sum(
        jnp.where(jnp.arange(row_count - 1, dtype=jnp.int32) == row_index - 1, mortar_shift, 0)
    )
    bands = state.shape[0]
    current = state
    band_ids = jnp.arange(bands, dtype=jnp.int32)
    for step in range(1, row_count + bands - 1):
        send_band = jnp.clip(step - 1 - row_index, 0, bands - 1)
        flux_one = lax.dynamic_index_in_dim(flux, send_band, 0, keepdims=False)
        state_one = lax.dynamic_index_in_dim(current, send_band, 0, keepdims=False)
        trace = jnp.dot(flux_one, state_one, precision=HIGH)[None]
        moved = turn_sectors(pass_down(trace), offset, levels)[0]
        band = step - row_index
        band_clip = jnp.clip(band, 0, bands - 1)
        lift_one = lax.dynamic_index_in_dim(lift, band_clip, 0, keepdims=False)
        solved_one = lax.dynamic_index_in_dim(state, band_clip, 0, keepdims=False)
        update = solved_one + jnp.dot(lift_one, moved, precision=HIGH)
        valid = jnp.logical_and(row_index >= 1, jnp.logical_and(band >= 0, band < bands))
        chosen = jnp.logical_and(valid, band_ids == band)[:, None, None]
        current = jnp.where(chosen, update[None], current)
    outlet = jnp.einsum("bfj,bjl->bfl", flux, current, precision=HIGH)
    return (current[None, None], outlet[None, None])


def solution(mesh):
    in_specs = (
        P("row", "sector", "band", None, None),
        P("row", "sector", "band", None, None),
        P("row", "sector", None, None),
        P("row", "sector", "band", None, None),
        P("row", "sector", "band", None, None),
        P(),
    )
    out_specs = (P("row", "sector", "band", None, None), P("row", "sector", "band", None, None))
    short = mesh.shape["sector"] <= RING_LIMIT and mesh.shape["row"] == 4
    on_device = ring_device if short else doubling_device
    return jax.shard_map(
        on_device, mesh=mesh, in_specs=in_specs, out_specs=out_specs, check_vma=False
    )
```

profile of v0, /device:TPU:7, one launch (start us, length us, event | category | flops | bytes accessed | tf_op | source)
XLA Modules:
  0.0 27.2 jit_solution(9155365052917609783)
XLA Ops:
  0.6 25.9 %ring.1 = (f32[320,128]{1,0:T(8,128)S(1)}, f32[80,128]{1,0:T(8,128)S(1)}) custom-call(s32[3]{0:T(128)} %shift_hbm.1, f32[320,128]{1,0:T(8,128)} %bitcast.11, f32[320,320]{1,0:T(8,128)} %bitcast.9, f32[320,320]{1,0:T(8,128)} %bitcast.10, f32[80,320]{1,0:T(8,128)} %bitcast.12, f32[80,320]{1,0:T(8,128)} %bitcast.13), custom_call_target="tpu_custom_call" | custom-call | tf_op jit(solution)/shard_map/ring/pallas_call | solution.py:373
  26.5 0.7 %leave.1 = (f32[320,128]{1,0:T(8,128)}, f32[80,128]{1,0:T(8,128)}) custom-call(f32[320,128]{1,0:T(8,128)S(1)} %get-tuple-element.6.corr_ref, f32[80,128]{1,0:T(8,128)S(1)} %get-tuple-element.7.out_ref), custom_call_target="tpu_custom_call" | custom-call | tf_op jit(solution)/shard_map/leave/pallas_call | solution.py:430
where the time goes:
time: 27.4 us; the launch traced here: 27.2 us
  Pallas kernels  26.6 us (97%)
  between operations  0.64 us (2%)
    pallas_call x1, Pallas kernels, ring_device(): pl.pallas_call(functools.partial(ring_kernel, sectors), out_shape=(pltpu....  25.9 us
    pallas_call x1, Pallas kernels, ring_device(): pl.pallas_call(leave_kernel, out_shape=(jax.ShapeDtypeStruct((blk, lines)...  0.69 us

commit v1 on v0

--- a/solution.py
+++ b/solution.py
@@ -78,7 +78,7 @@
     shift_ref, res, inv, coup, flux, lift, coup3, flux3, flow3, lift3, cross3, other3_a, other3_b,
     source, seen, state, landed, solved, trace, face_trace, final, above_a, above_b, beside_a, beside_b, crosses, stage, given,
     load_sem, send_sem, recv_sem, above_recv, beside_recv, trace_send,
-    cross_send, cross_recv, stage_send, given_recv,
+    cross_down_send, relay_send, cross_recv, stage_send, given_recv,
 ):
     row = lax.axis_index("row")
     sector = lax.axis_index("sector")
@@ -96,7 +96,7 @@
         )
 
     pairs = [
-        (flux_hbm, flux), (lift_hbm, lift), (inv_hbm, inv), (res_hbm, res), (coup_hbm, coup),
+        (inv_hbm, inv), (res_hbm, res), (coup_hbm, coup), (flux_hbm, flux), (lift_hbm, lift),
         (shift_hbm, shift_ref),
     ]
     loads = [
@@ -114,13 +114,10 @@
 
     greet(0, sectors - 1)
 
-    @pl.when(row == 1)
+    @pl.when(row % 2 == 1)
     def _():
         for k in range(1, sectors - 1):
             greet(0, k)
-
-    @pl.when(row % 2 == 1)
-    def _():
         for k in range(sectors):
             greet(1, k)
 
@@ -130,7 +127,7 @@
 
     loads[0].wait()
     loads[1].wait()
-    crosses[sector] = times(*split(flux[...]), lift[...].T)
+    source[...] = times(*split(inv[...]), res[...])
 
     @pl.when(row % 2 == 0)
     def _():
@@ -142,32 +139,7 @@
 
     @pl.when(row == 3)
     def _():
-        pl.semaphore_wait(barrier, 1)
-
-    def cross_copies():
-        return (
-            lambda: [
-                remote(crosses.at[sector], crosses.at[sector], cross_send.at[k], cross_recv.at[sector], 0, k)
-                for k in range(1, sectors)
-            ],
-            lambda: [
-                remote(crosses.at[sector], above_cross(sector), cross_send.at[k], cross_recv.at[sector], 1, k)
-                for k in range(sectors)
-            ],
-        )
-
-    def above_cross(k):
-        return crosses.at[sectors + k]
-
-    @pl.when(row == 1)
-    def _():
-        for copy in cross_copies()[0]():
-            copy.start()
-
-    @pl.when(row == 2)
-    def _():
-        for copy in cross_copies()[1]():
-            copy.start()
+        pl.semaphore_wait(barrier, sectors - 1)
 
     steps = sectors - 1
 
@@ -176,15 +148,61 @@
             state.at[k, q], landed.at[k, q], send_sem.at[k, q], recv_sem.at[k, q], 0, 1
         )
 
-    loads[2].wait()
-    loads[3].wait()
-    source[...] = times(*split(inv[...]), res[...])
     for q in range(QUARTERS):
         state[0, q] = pack(turn_lanes(source[...], -q * quarter), QUARTERS)
         ring_copy(0, q).start()
 
+    base = row // 2 * sectors
+
+    def cross_down():
+        return remote(
+            crosses.at[sector], crosses.at[sectors + sector], cross_down_send.at[0],
+            cross_recv.at[sector], 1, 0,
+        )
+
+    def relay_copy(side, j):
+        piece = turn(sectors - j) if side == 0 else turn(j)
+        return remote(
+            crosses.at[base + piece], crosses.at[base + piece], relay_send.at[side, j],
+            cross_recv.at[piece], 0, 1 if side == 0 else sectors - 1,
+        )
+
+    def has_piece(side, j):
+        return sector >= j if side == 0 else sector < sectors - j
+
+    def passes_on(side, j):
+        neighbour = sector < sectors - 1 if side == 0 else sector > 0
+        return jnp.logical_and(row % 2 == 1, jnp.logical_and(has_piece(side, j), neighbour))
+
+    def relay(j):
+        for side in range(2):
+            if j > 0:
+
+                @pl.when(jnp.logical_and(row % 2 == 1, has_piece(side, j)))
+                def _():
+                    relay_copy(side, j).wait_recv()
+
+            if j < sectors - 1:
+
+                @pl.when(passes_on(side, j))
+                def _():
+                    relay_copy(side, j).start()
+
+    loads[2].wait()
+    keep(coup3, coup[...])
+    loads[3].wait()
     loads[4].wait()
-    keep(coup3, coup[...])
+    crosses[sector] = times(*split(flux[...]), lift[...].T)
+
+    @pl.when(row == 2)
+    def _():
+        cross_down().start()
+
+    @pl.when(row == 3)
+    def _():
+        cross_down().wait_recv()
+
+    relay(0)
     loads[5].wait()
     shift = [shift_ref[i] for i in range(3)]
 
@@ -205,23 +223,19 @@
     def ready_other():
         @pl.when(row == 1)
         def _():
-            for i in range(1, sectors):
-                remote(
-                    crosses.at[turn(i)], crosses.at[turn(i)], cross_send.at[i],
-                    cross_recv.at[turn(i)], 0, i,
-                ).wait_recv()
             keep(other3[0], crosses[back(shift[1])])
             keep(other3[1], crosses[back(shift[1] + shift[2])])
 
         @pl.when(row == 3)
         def _():
-            for i in range(sectors):
-                remote(
-                    crosses.at[0], above_cross(i), cross_send.at[i], cross_recv.at[i], -1, i
-                ).wait_recv()
             keep(other3[0], crosses[sectors + back(shift[2])])
 
-    aside = [ready_flux, ready_flow, ready_lift, ready_other]
+    aside = [ready_flux, ready_flow]
+    for j in range(1, sectors):
+        aside.append(functools.partial(relay, j))
+        if j == 1:
+            aside.append(ready_lift)
+    aside.append(ready_other)
 
     def trace_copies(h):
         return (
@@ -283,7 +297,6 @@
         )
 
     def finish(h, moved):
-        moved = spread(moved, 2)
         final[h] = face_trace[h] + product(cross3, moved)
         solved[h] += product(lift3, moved)
 
@@ -301,26 +314,26 @@
                     beside_recv.at[h, turn(i)], 0, i,
                 ).wait_recv()
             beside[h][sector] = trace[h]
-            for i, by in enumerate((shift[1], shift[1] + shift[2])):
+            for i, by in ((1, shift[1] + shift[2]), (0, shift[1])):
                 moved = above[h][lax.rem(back(by) + sectors - shift[0], sectors)]
                 stage[h, i] = beside[h][back(by)] + pack(product(other3[i], spread(moved, 2)), 2)
                 stage_copy(h, i).start()
         for h in range(2):
-            finish(h, above[h][back(shift[0])])
+            finish(h, spread(above[h][back(shift[0])], 2))
 
     @pl.when(row == 2)
     def _():
         for h in range(2):
             stage_copy(h, 0).wait_recv()
-            finish(h, given[h])
+            finish(h, spread(given[h], 2))
 
     @pl.when(row == 3)
     def _():
         for h in range(2):
             wait_above(h)
+            moved = spread(above[h][back(shift[2])], 2)
             stage_copy(h, 1).wait_recv()
-            moved = above[h][back(shift[2])] + pack(product(other3[0], spread(given[h], 2)), 2)
-            finish(h, moved)
+            finish(h, moved + product(other3[0], spread(given[h], 2)))
 
     corr_ref[...] = join(solved[0], here(solved[1], 1), half)
     out_ref[...] = join(final[0], here(final[1], 1), half)
@@ -337,8 +350,6 @@
 
     @pl.when(row == 1)
     def _():
-        for copy in cross_copies()[0]():
-            copy.wait_send()
         for h in range(2):
             for copy in trace_copies(h)[1]():
                 copy.wait_send()
@@ -347,8 +358,14 @@
 
     @pl.when(row == 2)
     def _():
-        for copy in cross_copies()[1]():
-            copy.wait_send()
+        cross_down().wait_send()
+
+    for j in range(sectors - 1):
+        for side in range(2):
+
+            @pl.when(passes_on(side, j))
+            def _():
+                relay_copy(side, j).wait_send()
 
 
 def leave_kernel(corr_ref, out_ref, corr_hbm, out_hbm, sems):
@@ -410,7 +427,8 @@
             dma((2, sectors)),
             dma((2, sectors)),
             dma((2, sectors)),
-            dma((sectors,)),
+            dma((1,)),
+            dma((2, sectors)),
             dma((sectors,)),
             dma((2, 2)),
             dma((2,)),

time: 27.4 us -> 29.8 us (1.088)
  Pallas kernels: 26.6 us -> 28.8 us
    pallas_call x1, Pallas kernels: 25.9 us -> 28.1 us  [ring_device(): pl.pallas_call(functools.partial(ring_kernel, sectors), out_shape=(pltpu....]
where the time goes in v1:
time: 29.8 us; the launch traced here: 29.4 us
  Pallas kernels  28.8 us (97%)
  between operations  0.64 us (2%)
    pallas_call x1, Pallas kernels, ring_device(): pl.pallas_call(functools.partial(ring_kernel, sectors), out_shape=(pltpu....  28.1 us
    pallas_call x1, Pallas kernels, ring_device(): pl.pallas_call(leave_kernel, out_shape=(jax.ShapeDtypeStruct((blk, lines)...  0.69 us

profile of v1, /device:TPU:7, one launch (start us, length us, event | category | flops | bytes accessed | tf_op | source)
XLA Modules:
  0.0 29.4 jit_solution(16115715232369234135)
XLA Ops:
  0.6 28.1 %ring.1 = (f32[320,128]{1,0:T(8,128)S(1)}, f32[80,128]{1,0:T(8,128)S(1)}) custom-call(s32[3]{0:T(128)} %shift_hbm.1, f32[320,128]{1,0:T(8,128)} %bitcast.11, f32[320,320]{1,0:T(8,128)} %bitcast.9, f32[320,320]{1,0:T(8,128)} %bitcast.10, f32[80,320]{1,0:T(8,128)} %bitcast.12, f32[80,320]{1,0:T(8,128)} %bitcast.13), custom_call_target="tpu_custom_call" | custom-call | tf_op jit(solution)/shard_map/ring/pallas_call | solution.py:390
  28.7 0.7 %leave.1 = (f32[320,128]{1,0:T(8,128)}, f32[80,128]{1,0:T(8,128)}) custom-call(f32[320,128]{1,0:T(8,128)S(1)} %get-tuple-element.6.corr_ref, f32[80,128]{1,0:T(8,128)S(1)} %get-tuple-element.7.out_ref), custom_call_target="tpu_custom_call" | custom-call | tf_op jit(solution)/shard_map/leave/pallas_call | solution.py:448

commit v2 on v0

--- a/solution.py
+++ b/solution.py
@@ -96,7 +96,7 @@
         )
 
     pairs = [
-        (flux_hbm, flux), (lift_hbm, lift), (inv_hbm, inv), (res_hbm, res), (coup_hbm, coup),
+        (inv_hbm, inv), (res_hbm, res), (coup_hbm, coup), (flux_hbm, flux), (lift_hbm, lift),
         (shift_hbm, shift_ref),
     ]
     loads = [
@@ -130,7 +130,7 @@
 
     loads[0].wait()
     loads[1].wait()
-    crosses[sector] = times(*split(flux[...]), lift[...].T)
+    source[...] = times(*split(inv[...]), res[...])
 
     @pl.when(row % 2 == 0)
     def _():
@@ -159,16 +159,6 @@
     def above_cross(k):
         return crosses.at[sectors + k]
 
-    @pl.when(row == 1)
-    def _():
-        for copy in cross_copies()[0]():
-            copy.start()
-
-    @pl.when(row == 2)
-    def _():
-        for copy in cross_copies()[1]():
-            copy.start()
-
     steps = sectors - 1
 
     def ring_copy(k, q):
@@ -176,15 +166,26 @@
             state.at[k, q], landed.at[k, q], send_sem.at[k, q], recv_sem.at[k, q], 0, 1
         )
 
-    loads[2].wait()
-    loads[3].wait()
-    source[...] = times(*split(inv[...]), res[...])
     for q in range(QUARTERS):
         state[0, q] = pack(turn_lanes(source[...], -q * quarter), QUARTERS)
         ring_copy(0, q).start()
 
+    loads[2].wait()
+    keep(coup3, coup[...])
+    loads[3].wait()
     loads[4].wait()
-    keep(coup3, coup[...])
+    crosses[sector] = times(*split(flux[...]), lift[...].T)
+
+    @pl.when(row == 1)
+    def _():
+        for copy in cross_copies()[0]():
+            copy.start()
+
+    @pl.when(row == 2)
+    def _():
+        for copy in cross_copies()[1]():
+            copy.start()
+
     loads[5].wait()
     shift = [shift_ref[i] for i in range(3)]
 
@@ -221,7 +222,8 @@
                 ).wait_recv()
             keep(other3[0], crosses[sectors + back(shift[2])])
 
-    aside = [ready_flux, ready_flow, ready_lift, ready_other]
+    aside = {(0, 0): ready_flux, (0, 1): ready_flow, (0, 2): ready_lift}
+    last_aside = ready_other
 
     def trace_copies(h):
         return (
@@ -241,10 +243,11 @@
             came = product(coup3, spread(landed[k, q], QUARTERS))
             state[k + 1, q] = state[0, q] + pack(came, QUARTERS)
             ring_copy(k + 1, q).start()
-            if aside:
-                aside.pop(0)()
-    while aside:
-        aside.pop(0)()
+            if (k, q) in aside:
+                aside.pop((k, q))()
+    for left in aside.values():
+        left()
+    last_aside()
 
     def here(value, h):
         return turn_lanes(value, h * half)
@@ -283,7 +286,6 @@
         )
 
     def finish(h, moved):
-        moved = spread(moved, 2)
         final[h] = face_trace[h] + product(cross3, moved)
         solved[h] += product(lift3, moved)
 
@@ -301,26 +303,26 @@
                     beside_recv.at[h, turn(i)], 0, i,
                 ).wait_recv()
             beside[h][sector] = trace[h]
-            for i, by in enumerate((shift[1], shift[1] + shift[2])):
+            for i, by in ((1, shift[1] + shift[2]), (0, shift[1])):
                 moved = above[h][lax.rem(back(by) + sectors - shift[0], sectors)]
                 stage[h, i] = beside[h][back(by)] + pack(product(other3[i], spread(moved, 2)), 2)
                 stage_copy(h, i).start()
         for h in range(2):
-            finish(h, above[h][back(shift[0])])
+            finish(h, spread(above[h][back(shift[0])], 2))
 
     @pl.when(row == 2)
     def _():
         for h in range(2):
             stage_copy(h, 0).wait_recv()
-            finish(h, given[h])
+            finish(h, spread(given[h], 2))
 
     @pl.when(row == 3)
     def _():
         for h in range(2):
             wait_above(h)
+            moved = spread(above[h][back(shift[2])], 2)
             stage_copy(h, 1).wait_recv()
-            moved = above[h][back(shift[2])] + pack(product(other3[0], spread(given[h], 2)), 2)
-            finish(h, moved)
+            finish(h, moved + product(other3[0], spread(given[h], 2)))
 
     corr_ref[...] = join(solved[0], here(solved[1], 1), half)
     out_ref[...] = join(final[0], here(final[1], 1), half)

time: 27.4 us -> 26.7 us (0.974)
  Pallas kernels: 26.6 us -> 25.6 us
    pallas_call x1, Pallas kernels: 25.9 us -> 24.9 us  [ring_device(): pl.pallas_call(functools.partial(ring_kernel, sectors), out_shape=(pltpu....]
where the time goes in v2:
time: 26.7 us; the launch traced here: 26.3 us
  Pallas kernels  25.6 us (96%)
  between operations  0.64 us (2%)
    pallas_call x1, Pallas kernels, ring_device(): pl.pallas_call(functools.partial(ring_kernel, sectors), out_shape=(pltpu....  24.9 us
    pallas_call x1, Pallas kernels, ring_device(): pl.pallas_call(leave_kernel, out_shape=(jax.ShapeDtypeStruct((blk, lines)...  0.69 us

profile of v2, /device:TPU:7, one launch (start us, length us, event | category | flops | bytes accessed | tf_op | source)
XLA Modules:
  0.0 26.3 jit_solution(14684626034820239561)
XLA Ops:
  0.6 24.9 %ring.1 = (f32[320,128]{1,0:T(8,128)S(1)}, f32[80,128]{1,0:T(8,128)S(1)}) custom-call(s32[3]{0:T(128)} %shift_hbm.1, f32[320,128]{1,0:T(8,128)} %bitcast.11, f32[320,320]{1,0:T(8,128)} %bitcast.9, f32[320,320]{1,0:T(8,128)} %bitcast.10, f32[80,320]{1,0:T(8,128)} %bitcast.12, f32[80,320]{1,0:T(8,128)} %bitcast.13), custom_call_target="tpu_custom_call" | custom-call | tf_op jit(solution)/shard_map/ring/pallas_call | solution.py:375
  25.6 0.7 %leave.1 = (f32[320,128]{1,0:T(8,128)}, f32[80,128]{1,0:T(8,128)}) custom-call(f32[320,128]{1,0:T(8,128)S(1)} %get-tuple-element.6.corr_ref, f32[80,128]{1,0:T(8,128)S(1)} %get-tuple-element.7.out_ref), custom_call_target="tpu_custom_call" | custom-call | tf_op jit(solution)/shard_map/leave/pallas_call | solution.py:432

commit v3 on v2

--- a/solution.py
+++ b/solution.py
@@ -75,7 +75,7 @@
     sectors,
     shift_hbm, res_hbm, inv_hbm, coup_hbm, flux_hbm, lift_hbm,
     corr_ref, out_ref,
-    shift_ref, res, inv, coup, flux, lift, coup3, flux3, flow3, lift3, cross3, other3_a, other3_b,
+    shift_ref, res, inv, coup, flux, lift, coup3, flux3, flow3, end3, other3_a, other3_b,
     source, seen, state, landed, solved, trace, face_trace, final, above_a, above_b, beside_a, beside_b, crosses, stage, given,
     load_sem, send_sem, recv_sem, above_recv, beside_recv, trace_send,
     cross_send, cross_recv, stage_send, given_recv,
@@ -85,6 +85,7 @@
     above, beside, other3 = (above_a, above_b), (beside_a, beside_b), (other3_a, other3_b)
     lines = res.shape[1]
     quarter, half = lines // QUARTERS, lines // 2
+    depth, face = coup.shape[1], flux.shape[0]
 
     def turn(k):
         return lax.rem(sector + k, sectors)
@@ -197,11 +198,13 @@
         seen[...] = product(flux3, source[...])
 
     def ready_flow():
-        keep(flow3, times(*split(flux[...]), coup[...]))
+        flux_top, flux_rest = split(flux[...])
+        coup_top, coup_rest = coup3[:, :depth], coup3[:, 2 * depth :]
+        rest = dot(flux_top, coup_rest) + dot(flux_rest, coup_top)
+        keep(flow3, dot(flux_top, coup_top) + rest)
 
     def ready_lift():
-        keep(lift3, lift[...].T)
-        keep(cross3, crosses[sector])
+        keep(end3, jnp.concatenate([lift[...].T, crosses[sector]], axis=0))
 
     def ready_other():
         @pl.when(row == 1)
@@ -222,18 +225,21 @@
                 ).wait_recv()
             keep(other3[0], crosses[sectors + back(shift[2])])
 
-    aside = {(0, 0): ready_flux, (0, 1): ready_flow, (0, 2): ready_lift}
-    last_aside = ready_other
+    ready_flux()
+    last = QUARTERS - 1
+    aside = {(0, last - 1): ready_flow, (0, last): ready_lift, (1, last): ready_other}
+
+    far_first = sorted(range(1, sectors), key=lambda k: abs(2 * k - sectors)) + [0]
 
     def trace_copies(h):
         return (
             lambda: [
                 remote(trace.at[h], above[h].at[sector], trace_send.at[h, k], above_recv.at[h, sector], 1, k)
-                for k in range(sectors)
+                for k in far_first
             ],
             lambda: [
                 remote(trace.at[h], beside[h].at[sector], trace_send.at[h, k], beside_recv.at[h, sector], 0, k)
-                for k in range(1, sectors)
+                for k in far_first[:-1]
             ],
         )
 
@@ -247,7 +253,6 @@
                 aside.pop((k, q))()
     for left in aside.values():
         left()
-    last_aside()
 
     def here(value, h):
         return turn_lanes(value, h * half)
@@ -286,8 +291,9 @@
         )
 
     def finish(h, moved):
-        final[h] = face_trace[h] + product(cross3, moved)
-        solved[h] += product(lift3, moved)
+        both = product(end3, moved)
+        solved[h] += both[:depth]
+        final[h] = face_trace[h] + both[depth:]
 
     @pl.when(row == 0)
     def _():
@@ -387,8 +393,7 @@
             pltpu.VMEM((blk, 3 * blk), BF16),
             pltpu.VMEM((face, 3 * blk), BF16),
             pltpu.VMEM((face, 3 * blk), BF16),
-            pltpu.VMEM((blk, 3 * face), BF16),
-            pltpu.VMEM((face, 3 * face), BF16),
+            pltpu.VMEM((blk + face, 3 * face), BF16),
             pltpu.VMEM((face, 3 * face), BF16),
             pltpu.VMEM((face, 3 * face), BF16),
             pltpu.VMEM((blk, lines), F32),

time: 26.7 us -> 26.7 us (level)
  no operation moved by 1% of the time
where the time goes in v3:
time: 26.7 us; the launch traced here: 26.3 us
  Pallas kernels  25.7 us (96%)
  between operations  0.64 us (2%)
    pallas_call x1, Pallas kernels, ring_device(): pl.pallas_call(functools.partial(ring_kernel, sectors), out_shape=(pltpu....  25 us
    pallas_call x1, Pallas kernels, ring_device(): pl.pallas_call(leave_kernel, out_shape=(jax.ShapeDtypeStruct((blk, lines)...  0.69 us

profile of v3, /device:TPU:7, one launch (start us, length us, event | category | flops | bytes accessed | tf_op | source)
XLA Modules:
  0.0 26.3 jit_solution(6599999215857736063)
XLA Ops:
  0.6 25.0 %ring.1 = (f32[320,128]{1,0:T(8,128)S(1)}, f32[80,128]{1,0:T(8,128)S(1)}) custom-call(s32[3]{0:T(128)} %shift_hbm.1, f32[320,128]{1,0:T(8,128)} %bitcast.11, f32[320,320]{1,0:T(8,128)} %bitcast.9, f32[320,320]{1,0:T(8,128)} %bitcast.10, f32[80,320]{1,0:T(8,128)} %bitcast.12, f32[80,320]{1,0:T(8,128)} %bitcast.13), custom_call_target="tpu_custom_call" | custom-call | tf_op jit(solution)/shard_map/ring/pallas_call | solution.py:381
  25.7 0.7 %leave.1 = (f32[320,128]{1,0:T(8,128)}, f32[80,128]{1,0:T(8,128)}) custom-call(f32[320,128]{1,0:T(8,128)S(1)} %get-tuple-element.6.corr_ref, f32[80,128]{1,0:T(8,128)S(1)} %get-tuple-element.7.out_ref), custom_call_target="tpu_custom_call" | custom-call | tf_op jit(solution)/shard_map/leave/pallas_call | solution.py:437

commit v4 on v3

--- a/solution.py
+++ b/solution.py
@@ -96,10 +96,13 @@
             device_id={"row": row + down, "sector": turn(k)}, device_id_type=MESH,
         )
 
+    high = inv.shape[0] // QUARTERS
+    blocks = [pl.ds(i * high, high) for i in range(QUARTERS)]
     pairs = [
-        (inv_hbm, inv), (res_hbm, res), (coup_hbm, coup), (flux_hbm, flux), (lift_hbm, lift),
+        (res_hbm, res), (coup_hbm, coup), (flux_hbm, flux), (lift_hbm, lift),
         (shift_hbm, shift_ref),
     ]
+    pairs[1:1] = [(inv_hbm.at[block], inv.at[block]) for block in blocks]
     loads = [
         pltpu.make_async_copy(src, dst, load_sem.at[i]) for i, (src, dst) in enumerate(pairs)
     ]
@@ -129,9 +132,10 @@
     def _():
         greet(row - 1, 0)
 
-    loads[0].wait()
-    loads[1].wait()
-    source[...] = times(*split(inv[...]), res[...])
+    loads.pop(0).wait()
+    for block in blocks:
+        loads.pop(0).wait()
+        source[block] = times(*split(inv[block]), res[...])
 
     @pl.when(row % 2 == 0)
     def _():
@@ -171,10 +175,10 @@
         state[0, q] = pack(turn_lanes(source[...], -q * quarter), QUARTERS)
         ring_copy(0, q).start()
 
+    loads[0].wait()
+    keep(coup3, coup[...])
+    loads[1].wait()
     loads[2].wait()
-    keep(coup3, coup[...])
-    loads[3].wait()
-    loads[4].wait()
     crosses[sector] = times(*split(flux[...]), lift[...].T)
 
     @pl.when(row == 1)
@@ -187,7 +191,7 @@
         for copy in cross_copies()[1]():
             copy.start()
 
-    loads[5].wait()
+    loads[3].wait()
     shift = [shift_ref[i] for i in range(3)]
 
     def back(by):
@@ -411,7 +415,7 @@
             pltpu.VMEM((2 * sectors, face, face), F32),
             pltpu.VMEM((2, 2, face // 2, lines), F32),
             pltpu.VMEM((2, face // 2, lines), F32),
-            dma((6,)),
+            dma((QUARTERS + 5,)),
             dma((steps, QUARTERS)),
             dma((steps, QUARTERS)),
             dma((2, sectors)),

time: 26.7 us -> 27 us (1.011)
  Pallas kernels: 25.7 us -> 26 us
    pallas_call x1, Pallas kernels: 25 us -> 25.3 us  [ring_device(): pl.pallas_call(functools.partial(ring_kernel, sectors), out_shape=(pltpu....]
where the time goes in v4:
time: 27 us; the launch traced here: 26.7 us
  Pallas kernels  26 us (96%)
  between operations  0.64 us (2%)
    pallas_call x1, Pallas kernels, ring_device(): pl.pallas_call(functools.partial(ring_kernel, sectors), out_shape=(pltpu....  25.3 us
    pallas_call x1, Pallas kernels, ring_device(): pl.pallas_call(leave_kernel, out_shape=(jax.ShapeDtypeStruct((blk, lines)...  0.69 us

profile of v4, /device:TPU:7, one launch (start us, length us, event | category | flops | bytes accessed | tf_op | source)
XLA Modules:
  0.0 26.7 jit_solution(4446020024693044089)
XLA Ops:
  0.6 25.3 %ring.1 = (f32[320,128]{1,0:T(8,128)S(1)}, f32[80,128]{1,0:T(8,128)S(1)}) custom-call(s32[3]{0:T(128)} %shift_hbm.1, f32[320,128]{1,0:T(8,128)} %bitcast.11, f32[320,320]{1,0:T(8,128)} %bitcast.9, f32[320,320]{1,0:T(8,128)} %bitcast.10, f32[80,320]{1,0:T(8,128)} %bitcast.12, f32[80,320]{1,0:T(8,128)} %bitcast.13), custom_call_target="tpu_custom_call" | custom-call | tf_op jit(solution)/shard_map/ring/pallas_call | solution.py:385
  26.0 0.7 %leave.1 = (f32[320,128]{1,0:T(8,128)}, f32[80,128]{1,0:T(8,128)}) custom-call(f32[320,128]{1,0:T(8,128)S(1)} %get-tuple-element.6.corr_ref, f32[80,128]{1,0:T(8,128)S(1)} %get-tuple-element.7.out_ref), custom_call_target="tpu_custom_call" | custom-call | tf_op jit(solution)/shard_map/leave/pallas_call | solution.py:441
